TPU v7x, 32 devices: a whole 2x2x4 slice. The times are simulated.
32 devices in a mesh: row: 4 (over y, core), col: 8 (over z, x).
Axes of the slice: x: 2, y: 2, z: 4, core: 2. Of those that a mesh axis runs over, the one named last changes fastest.
Arguments:
- band: float32 [8, 4, 4, 8, 512, 512], P(None, 'row', None, 'col'), as said below
Outputs:
- factored: float32 [8, 4, 4, 8, 512, 512], P(None, 'row', None, 'col')
Inputs may be any that keep to these rules, and one draw needn't show every extreme that they name: band holds the tiles of a symmetric matrix; its diagonal tiles are symmetric positive definite, and those of tile columns 0 and 1 leave every pivot of the steps positive.
All inputs are finite; a program needn't handle non-finite values.
Results may differ from a plain program's by a relative error of at most 0.00015.
Values sent between devices are 32-bit elements; how exact they have to be, the bound alone decides.
A program may use at most 192 MiB of HBM per device.

v0:
```python
import jax
import jax.numpy as jnp
from jax import lax
from jax.sharding import PartitionSpec as P

BANDT = 32
STEPS = 2


def spread(x, axis, root):
    mine = lax.axis_index(axis) == root
    return lax.psum(jnp.where(mine, x, jnp.zeros_like(x)), axis)


def shards(band):
    slots, _, colgroups, _, tile, _ = band.shape
    grid_rows = lax.axis_size("row")
    grid_cols = lax.axis_size("col")
    my_row = lax.axis_index("row")
    my_col = lax.axis_index("col")
    highest = lax.Precision.HIGHEST
    local = band.reshape(slots, colgroups, tile, tile)
    slot_ids = jnp.arange(slots, dtype=jnp.int32)[:, None]
    columns_here = jnp.arange(colgroups, dtype=jnp.int32)[None, :] * grid_cols + my_col
    offsets_here = slot_ids * grid_rows + (my_row - columns_here) % grid_rows
    rows_here = columns_here + offsets_here
    identity = jnp.eye(tile, dtype=jnp.float32)
    for step in range(STEPS):
        root_col = step % grid_cols
        root_row = step % grid_rows
        group_slot = step // grid_cols
        column = local[:, group_slot]
        factor = jnp.linalg.cholesky(column[0])
        inverse = lax.linalg.triangular_solve(factor, identity, left_side=True, lower=True)
        panel_offsets = jnp.arange(slots, dtype=jnp.int32) * grid_rows + (my_row - step) % grid_rows
        is_diagonal = (panel_offsets == 0)[:, None, None]
        inverse = spread(inverse, "row", root_row)
        applied = jnp.einsum("sab,cb->sac", column, inverse, precision=highest)
        stored = jnp.where(is_diagonal, factor, applied)
        slab = spread(stored, "col", root_col)
        local = local.at[:, group_slot].set(jnp.where(my_col == root_col, stored, column))
        picked = []
        for group_index in range(colgroups):
            target = group_index * grid_cols + my_col
            position = jnp.clip((target - step) // grid_rows, 0, slots - 1)
            candidate = lax.dynamic_index_in_dim(slab, position, 0, keepdims=False)
            picked.append(spread(candidate, "row", target % grid_rows))
        across = jnp.stack(picked)
        wanted = jnp.clip((rows_here - step) // grid_rows, 0, slots - 1)
        active = (columns_here >= step + 1) & (rows_here <= step + BANDT - 1)
        gathered = jnp.take(slab, wanted.reshape(-1), axis=0).reshape(slots, colgroups, tile, tile)
        update = jnp.einsum("sqab,qcb->sqac", gathered, across, precision=highest)
        local = local - jnp.where(active[:, :, None, None], update, 0.0)
    return local.reshape(slots, 1, colgroups, 1, tile, tile)


def solution(mesh):
    return jax.shard_map(
        shards,
        mesh=mesh,
        in_specs=(P(None, "row", None, "col", None, None),),
        out_specs=P(None, "row", None, "col", None, None),
        check_vma=False,
    )
```

profile of v0, /device:TPU:3, one launch (start us, length us, event | category | flops | bytes accessed | tf_op | source)
XLA Modules:
  0.0 1342.6 jit_solution(1134901533301925404)
XLA Ops:
  6.7 34.3 %copy.19 = f32[8,1,4,1,512,512]{4,5,0,2,3,1:T(8,128)} copy(f32[8,1,4,1,512,512]{5,4,3,2,1,0:T(8,128)} %param.10) | data formatting | bytes 67108864 | tf_op args[0]
  40.9 1.3 slice_bitcast_fusion.5
  42.6 1.4 fusion.19
  44.0 11.7 cholesky.286
  55.9 9.8 custom-call.27
  66.4 11.7 cholesky.305
  78.2 10.1 custom-call.28
  89.0 11.7 cholesky.326
  100.7 9.8 custom-call.29
  111.1 11.7 cholesky.343
  127.5 1.4 fusion.23
  128.9 11.2 while.6
  129.5 2.2 bitcast_dynamic-update-slice_fusion.6
  132.4 2.2 bitcast_dynamic-update-slice_fusion.6
  135.2 2.2 bitcast_dynamic-update-slice_fusion.6
  138.0 2.1 bitcast_dynamic-update-slice_fusion.6
  140.2 39.3 %custom-call.30 = f32[4,128,128]{1,2,0:T(8,128)S(1)} custom-call(f32[4,128,128]{2,1,0:T(8,128)S(1)} %get-tuple-element.46), custom_call_target="InvertDiagBlocksLowerTriangular" | custom-call | tf_op jit(solution)/shard_map/triangular_solve/custom-call.3 | solution.py:34
  179.9 1.2 convolution_subtract_fusion.3
  181.6 1.3 convolution_subtract_fusion.2
  183.3 1.6 convolution_subtract_fusion.5
  185.3 1.1 maximum_select_fusion
  186.9 36.6 %all-reduce.10.cloned.1.call-done = f32[512,512]{1,0:T(8,128)} async-done(((f32[512,512]{1,0:T(8,128)}), f32[512,512]{1,0:T(8,128)}) %all-reduce.10.cloned.1.call-update) | async-done | bytes 1048592 | tf_op jit(solution)/shard_map/psum | solution.py:12
  223.5 19.8 %fusion.3 = (f32[8,512,512]{1,2,0:T(8,128)}, f32[512,8,512]{2,0,1:T(8,128)}) fusion(f32[512,512]{0,1:T(8,128)S(1)} %copy.21, pred[8]{0:T(512)(128)(4,1)S(1)} %add_compare_fusion.1, pred[]{:T(512)S(6)} %eq.62, f32[8,4,512,512]{2,3,0,1:T(8,128)} %bitcast.172, f32[512,512]{1,0:T(8,128)} %all-reduce.10.cloned.1.call-done), kind=kOutput, calls=%fused_computation.18 | convolution fusion | flops 12889096192 | bytes 27262984 | tf_op jit(solution)/shard_map/sab,cb->sac/dot_general | solution.py:38
  244.8 8.1 slice_bitcast_fusion.1
  252.9 11.5 bitcast_dynamic-update-slice_fusion.3
  264.4 250.3 %all-reduce.12.cloned.1.call-done = f32[8,512,512]{1,2,0:T(8,128)} async-done(((f32[8,512,512]{1,2,0:T(8,128)}), f32[8,512,512]{1,2,0:T(8,128)}) %all-reduce.12.cloned.1.call-update) | async-done | bytes 8388624 | tf_op jit(solution)/shard_map/psum | solution.py:12
  514.7 4.4 dynamic-slice_select_fusion.7
  519.1 16.5 %gather_fusion = f32[32,512,512]{1,2,0:T(8,128)} fusion(f32[8,512,512]{1,2,0:T(8,128)} %all-reduce.12.cloned.1.call-done, s32[1024]{0:T(1024)S(1)} %pad_clamp_fusion.1), kind=kCustom, calls=%fused_computation.clone | custom fusion | bytes 67108992 | tf_op jit(solution)/shard_map/jit(_take)/gather | solution.py:51
  535.6 23.6 %broadcast_select_fusion.1 = f32[32,512,512]{1,2,0:T(8,128)} fusion(f32[32,512,512]{1,2,0:T(8,128)} %gather_fusion, pred[32]{0:T(512)(128)(4,1)S(1)} %get-tuple-element.114), kind=kLoop, calls=%fused_computation.12 | loop fusion | flops 8388608 | bytes 67108896 | tf_op jit(solution)/shard_map/jit(_take)/select_n | solution.py:51
  559.3 44.9 %all-reduce.20.cloned.1.call-done = (f32[1,512,512]{1,2,0:T(8,128)}, f32[1,512,512]{1,2,0:T(8,128)}, f32[1,512,512]{1,2,0:T(8,128)}, f32[1,512,512]{1,2,0:T(8,128)}) async-done(((f32[1,512,512]{1,2,0:T(8,128)}, f32[1,512,512]{1,2,0:T(8,128)}, f32[1,512,512]{1,2,0:T(8,128)}, f32[1,512,512]{1,2,0:T(8,128)}), (f32[1,512,512]{1,2,0:T(8,128)}, f32[1,512,512]{1,2,0:T(8,128)}, f32[1,512,512]{1,2,0:T(8,128)}, ...) | async-done | bytes 4194320 | tf_op jit(solution)/shard_map/psum | solution.py:12
  604.2 2.6 maximum_bitcast_fusion.9
  606.8 63.8 %fusion.2 = f32[8,4,512,512]{2,3,1,0:T(8,128)} fusion(f32[8,4,512,512]{2,3,0,1:T(8,128)} %bitcast_dynamic-update-slice_fusion.3, pred[8,4]{1,0:T(8,128)(4,1)S(1)} %get-tuple-element.113, f32[8,4,512,512]{2,3,1,0:T(8,128)} %bitcast.176, f32[4,512,512,1]{1,2,0,3:T(8,128)S(1)} %maximum_bitcast_fusion.9), kind=kOutput, calls=%fused_computation.10 | convolution fusion | flops 51556384768 | bytes 104857632 | tf_op jit(solution)/shard_map/sqab,qcb->sqac/dot_general | solution.py:52
  670.6 1.3 slice_bitcast_fusion.4
  672.3 1.4 fusion.18
  673.8 11.7 cholesky.358
  685.6 9.8 custom-call.31
  696.1 11.7 cholesky.377
  707.9 10.2 custom-call.32
  718.7 11.7 cholesky.398
  730.5 9.8 custom-call.33
  740.9 11.7 cholesky.415
  758.0 1.4 fusion.22
  759.4 11.8 while.7
  760.1 2.3 bitcast_dynamic-update-slice_fusion.7
  763.0 2.3 bitcast_dynamic-update-slice_fusion.7
  766.0 2.3 bitcast_dynamic-update-slice_fusion.7
  768.9 2.2 bitcast_dynamic-update-slice_fusion.7
  771.2 39.3 %custom-call.34 = f32[4,128,128]{1,2,0:T(8,128)S(1)} custom-call(f32[4,128,128]{2,1,0:T(8,128)S(1)} %get-tuple-element.47), custom_call_target="InvertDiagBlocksLowerTriangular" | custom-call | tf_op jit(solution)/shard_map/triangular_solve/custom-call.3 | solution.py:34
  810.9 1.2 convolution_subtract_fusion.1
  812.6 1.3 convolution_subtract_fusion
  814.3 1.6 convolution_subtract_fusion.4
  816.3 1.1 maximum_select_fusion.1
  817.9 35.5 %all-reduce.14.cloned.1.call-done = f32[512,512]{1,0:T(8,128)} async-done(((f32[512,512]{1,0:T(8,128)}), f32[512,512]{1,0:T(8,128)}) %all-reduce.14.cloned.1.call-update) | async-done | bytes 1048592 | tf_op jit(solution)/shard_map/psum | solution.py:12
  853.3 20.7 %select_select_fusion = (f32[8,512,512]{1,2,0:T(8,128)}, f32[8,512,512]{1,2,0:T(8,128)}) fusion(f32[512,512]{0,1:T(8,128)S(1)} %copy.28, pred[8]{0:T(512)(128)(4,1)S(1)} %add_compare_fusion, pred[]{:T(512)S(6)} %eq.70, f32[512,512]{1,0:T(8,128)} %all-reduce.14.cloned.1.call-done, f32[8,4,512,512]{2,3,1,0:T(8,128)} %fusion.2), kind=kOutput, calls=%fused_computation.21 | convolution fusion | flops 12889096192 | bytes 27262984 | tf_op jit(solution)/shard_map/sab,cb->sac/dot_general | solution.py:38
  874.1 8.1 slice_bitcast_fusion
  882.3 9.0 bitcast_dynamic-update-slice_fusion.2
  891.2 254.2 %all-reduce.16.cloned.1.call-done = f32[8,512,512]{1,2,0:T(8,128)} async-done(((f32[8,512,512]{1,2,0:T(8,128)}), f32[8,512,512]{1,2,0:T(8,128)}) %all-reduce.16.cloned.1.call-update) | async-done | bytes 8388624 | tf_op jit(solution)/shard_map/psum | solution.py:12
  1145.4 4.4 dynamic-slice_select_fusion.3
  1149.8 17.1 %gather_fusion.1 = f32[32,512,512]{1,2,0:T(8,128)} fusion(f32[8,512,512]{1,2,0:T(8,128)} %all-reduce.16.cloned.1.call-done, s32[1024]{0:T(1024)S(1)} %pad_clamp_fusion), kind=kCustom, calls=%fused_computation.1.clone | custom fusion | bytes 67108992 | tf_op jit(solution)/shard_map/jit(_take)/gather | solution.py:51
  1166.8 23.7 %broadcast_select_fusion = f32[32,512,512]{1,2,0:T(8,128)} fusion(f32[32,512,512]{1,2,0:T(8,128)} %gather_fusion.1, pred[32]{0:T(512)(128)(4,1)S(1)} %get-tuple-element.72), kind=kLoop, calls=%fused_computation.11 | loop fusion | flops 8388608 | bytes 67108896 | tf_op jit(solution)/shard_map/jit(_take)/select_n | solution.py:51
  1190.6 44.3 %all-reduce.18.cloned.1.call-done = (f32[1,512,512]{1,2,0:T(8,128)}, f32[1,512,512]{1,2,0:T(8,128)}, f32[1,512,512]{1,2,0:T(8,128)}, f32[1,512,512]{1,2,0:T(8,128)}) async-done(((f32[1,512,512]{1,2,0:T(8,128)}, f32[1,512,512]{1,2,0:T(8,128)}, f32[1,512,512]{1,2,0:T(8,128)}, f32[1,512,512]{1,2,0:T(8,128)}), (f32[1,512,512]{1,2,0:T(8,128)}, f32[1,512,512]{1,2,0:T(8,128)}, f32[1,512,512]{1,2,0:T(8,128)}, ...) | async-done | bytes 4194320 | tf_op jit(solution)/shard_map/psum | solution.py:12
  1234.9 2.6 maximum_bitcast_fusion.8
  1237.5 63.8 %fusion.1 = f32[8,1,4,1,512,512]{4,5,2,0,3,1:T(8,128)} fusion(f32[8,4,512,512]{2,3,1,0:T(8,128)} %bitcast_dynamic-update-slice_fusion.2, pred[8,4]{1,0:T(8,128)(4,1)S(1)} %copy-done, f32[8,4,512,512]{2,3,1,0:T(8,128)} %bitcast.175, f32[4,512,512,1]{1,2,0,3:T(8,128)S(1)} %maximum_bitcast_fusion.8), kind=kOutput, calls=%fused_computation.8 | convolution fusion | flops 51556384768 | bytes 104857632 | tf_op jit(solution)/shard_map/sqab,qcb->sqac/dot_general | solution.py:52
  1301.3 34.1 %copy.35 = f32[8,1,4,1,512,512]{5,4,3,2,1,0:T(8,128)} copy(f32[8,1,4,1,512,512]{4,5,2,0,3,1:T(8,128)} %fusion.1) | data formatting | bytes 67108864 | tf_op jit(solution)/shard_map/reshape | solution.py:54
  (94 shorter events, 20.6 us)
Async XLA Ops:
  6.5 217.0 %all-reduce.10.cloned.1.call-start = ((), (), s32[]{:S(2)}) async-start(), calls=%async_computation | async-start | bytes 2097152 | tf_op jit(solution)/shard_map/psum | solution.py:12
  186.5 328.2 %all-reduce.12.cloned.1.call-start = ((), (), s32[]{:S(2)}) async-start(), calls=%async_computation.1 | async-start | bytes 16777216 | tf_op jit(solution)/shard_map/psum | solution.py:12
  243.4 360.9 %all-reduce.20.cloned.1.call-start = ((), (), s32[]{:S(2)}) async-start(), calls=%async_computation.5 | async-start | bytes 8388608 | tf_op jit(solution)/shard_map/psum | solution.py:12
  519.1 334.2 %all-reduce.14.cloned.1.call-start = ((), (), s32[]{:S(2)}) async-start(), calls=%async_computation.2 | async-start | bytes 2097152 | tf_op jit(solution)/shard_map/psum | solution.py:12
  817.4 327.9 %all-reduce.16.cloned.1.call-start = ((), (), s32[]{:S(2)}) async-start(), calls=%async_computation.3 | async-start | bytes 16777216 | tf_op jit(solution)/shard_map/psum | solution.py:12
  874.0 360.8 %all-reduce.18.cloned.1.call-start = ((), (), s32[]{:S(2)}) async-start(), calls=%async_computation.4 | async-start | bytes 8388608 | tf_op jit(solution)/shard_map/psum | solution.py:12
  1190.6 46.9 %copy-start = (pred[8,4]{1,0:T(8,128)(4,1)S(1)}, pred[8,4]{1,0:T(8,128)(4,1)}, u32[]{:S(2)}) copy-start(pred[8,4]{1,0:T(8,128)(4,1)} %get-tuple-element.112) | copy-start | bytes 100
Sparse Core Ops, SparseCore 0:
  186.6 36.8 all-reduce.9
  243.5 271.1 all-reduce.11
  519.2 84.9 all-reduce.19
  817.6 35.7 all-reduce.13
  874.2 271.1 all-reduce.15
  1149.9 84.9 all-reduce.17
where the time goes:
time: 1360 us; the launch traced here: 1340 us
  waiting for transfers between devices  666 us (49%)
  other arithmetic  328 us (24%)
  matrix products  183 us (13%)
  local copies, waits for them, and re-layouts  145 us (11%)
  between operations  19.6 us (1%)
    psum x6, waiting for transfers between devices, spread(): return lax.psum(jnp.where(mine, x, jnp.zeros_like(x)), axis)  666 us
    another operation x29, other arithmetic, shards(): factor = jnp.linalg.cholesky(column[0])  158 us
    dot_general x2, matrix products, shards(): update = jnp.einsum('sqab,qcb->sqac', gathered, across, precision=highest)  128 us
    another operation x5, other arithmetic, shards(): lax.linalg.triangular_solve(factor, identity, left_side=True, lower=True)  81.4 us
    select_n x2, other arithmetic, shards(): jnp.take(slab, wanted.reshape(-1), axis=0)  47.4 us
    dot_general x2, matrix products, shards(): applied = jnp.einsum('sab,cb->sac', column, inverse, precision=highest)  40.5 us
    unnamed x3, local copies, waits for them, and re-layouts  34.3 us
    reshape x1, local copies, waits for them, and re-layouts, shards(): return local.reshape(slots, 1, colgroups, 1, tile, tile)  34.1 us
  transfers between devices with their start and end apart: 6, of which 6 were waited for; matrix products, arithmetic and copies ran while one was open for 9% of the time, Pallas kernels for 0%

commit v1 on v0

v1 whole, which is shorter than its diff:
```python
import functools

import jax
import jax.numpy as jnp
from jax import lax
from jax.experimental import pallas as pl
from jax.experimental.pallas import tpu as pltpu
from jax.sharding import PartitionSpec as P

STEPS = 2
BLOCK = 128
MESH = pl.DeviceIdType.MESH
NT = (((1,), (1,)), ((), ()))
NN = (((1,), (0,)), ((), ()))


def exact(a, b, dims):
    return lax.dot_general(a, b, dims, precision=lax.Precision.HIGHEST, preferred_element_type=jnp.float32)


def split(x):
    hi = x.astype(jnp.bfloat16)
    return hi, (x - hi.astype(jnp.float32)).astype(jnp.bfloat16)


def three(ah, al, bh, bl):
    dot = functools.partial(lax.dot_general, dimension_numbers=NT, preferred_element_type=jnp.float32)
    return dot(ah, bh) + (dot(ah, bl) + dot(al, bh))


def spread_kernel(band, rows, seeds, chain_send, chain_recv, peer_send, peer_recv, across_send, across_recv, across_own,
                  seed_send, seed_recv):
    n = lax.axis_size("row")
    grid_cols = lax.axis_size("col")
    slots, groups = band.shape[:2]
    r = lax.axis_index("row")
    c = lax.axis_index("col")
    lane = lax.rem(c, STEPS)
    other = 1 - lane
    peer = c + 1 - 2 * lane
    first = c < STEPS
    last = c >= grid_cols - STEPS
    before = jnp.where(first, c, c - STEPS)
    after = jnp.where(last, c, c + STEPS)
    place = lax.rem(r - lax.rem(c, n) + n, n)
    below = lax.rem(r + 1, n)

    barrier = pltpu.get_barrier_semaphore()

    @pl.when(jnp.logical_not(first))
    def _():
        pl.semaphore_signal(barrier, inc=1, device_id=(r, before), device_id_type=MESH)

    @pl.when(jnp.logical_not(last))
    def _():
        pl.semaphore_signal(barrier, inc=1, device_id=(r, after), device_id_type=MESH)

    pl.semaphore_signal(barrier, inc=1, device_id=(r, peer), device_id_type=MESH)
    for hop in range(1, n):
        pl.semaphore_signal(barrier, inc=1, device_id=(lax.rem(r + hop, n), c), device_id_type=MESH)
    pl.semaphore_wait(barrier, n + jnp.where(first, 0, 1) + jnp.where(last, 0, 1))

    @pl.when(first)
    def _():
        @pl.loop(0, slots)
        def _(s):
            pltpu.make_async_copy(band.at[s, 0], rows.at[lane, s], chain_recv.at[s]).start()

    def chain_copy(s):
        return pltpu.make_async_remote_copy(
            rows.at[lane, s], rows.at[lane, s], chain_send.at[s], chain_recv.at[s],
            device_id=(r, after), device_id_type=MESH)

    def peer_copy(s, which):
        return pltpu.make_async_remote_copy(
            rows.at[which, s], rows.at[which, s], peer_send.at[s], peer_recv.at[s],
            device_id=(r, peer), device_id_type=MESH)

    def across_copy(k, g, source):
        return pltpu.make_async_remote_copy(
            rows.at[k, source], rows.at[k, slots + g], across_send.at[k, g], across_recv.at[k, g],
            device_id=(below, c), device_id_type=MESH)

    def own_copy(k, g, source):
        return pltpu.make_async_copy(rows.at[k, source], rows.at[k, slots + g], across_own.at[k, g])

    def seed_copy(k, which, hop):
        return pltpu.make_async_remote_copy(
            rows.at[k, 0], seeds.at[which], seed_send.at[which, hop], seed_recv.at[which],
            device_id=(lax.rem(r + hop, n), c), device_id_type=MESH)

    def source_slot(k, g):
        return jnp.clip((g * grid_cols + c - k + n) // n - 1, 0, slots - 1)

    seed_list = ((0, 0, 0), (0, 1, 1), (1, 1, 2))

    def receive(s):
        chain_copy(s).wait_recv()

        @pl.when(jnp.logical_not(last))
        def _():
            chain_copy(s).start()

        peer_copy(s, lane).start()

    def pass_on(s):
        peer_copy(s, other).wait_recv()
        for k in range(STEPS):
            for g in range(groups):
                slot = source_slot(k, g)

                @pl.when(jnp.logical_and(place == 0, slot == s))
                def _():
                    across_copy(k, g, s).start()
                    own_copy(k, g, s).start()

    receive(0)
    pass_on(0)
    for k, root, which in seed_list:
        @pl.when(r == root)
        def _():
            for hop in range(1, n):
                seed_copy(k, which, hop).start()
            pltpu.make_async_copy(rows.at[k, 0], seeds.at[which], seed_recv.at[which]).start()

    receive(1)

    @pl.loop(2, slots)
    def _(s):
        receive(s)
        pass_on(s - 1)

    pass_on(slots - 1)

    for g in range(groups):
        for k in range(STEPS):
            @pl.when(place > 0)
            def _():
                across_copy(k, g, slots + g).wait_recv()

                @pl.when(place < n - 1)
                def _():
                    across_copy(k, g, slots + g).start()

    for k, root, which in seed_list:
        seed_copy(k, which, 1).wait_recv()

        @pl.when(r == root)
        def _():
            for hop in range(1, n):
                seed_copy(k, which, hop).wait_send()

    for g in range(groups):
        for k in range(STEPS):
            @pl.when(place == 0)
            def _():
                own_copy(k, g, 0).wait()

            @pl.when(place < n - 1)
            def _():
                across_copy(k, g, slots + g).wait_send()

    @pl.loop(0, slots)
    def _(s):
        peer_copy(s, lane).wait_send()

        @pl.when(jnp.logical_not(last))
        def _():
            chain_copy(s).wait_send()


def factor_block(block):
    size = block.shape[0]
    row_ids = lax.broadcasted_iota(jnp.int32, (size, size), 0)
    lane_ids = lax.broadcasted_iota(jnp.int32, (size, size), 1)
    eye = (row_ids == lane_ids).astype(jnp.float32)

    def eliminate(k, carry):
        left, right = carry
        column = jnp.sum(jnp.where(lane_ids == k, left, 0.0), axis=1, keepdims=True)
        here = row_ids == k
        row_left = jnp.sum(jnp.where(here, left, 0.0), axis=0, keepdims=True)
        row_right = jnp.sum(jnp.where(here, right, 0.0), axis=0, keepdims=True)
        pivot = jnp.sum(jnp.where(lane_ids[:1] == k, row_left, 0.0), axis=1, keepdims=True)
        column = jnp.where(row_ids[:, :1] > k, column, 0.0)
        scale = 1.0 / pivot
        return left - column * (row_left * scale), right - column * (row_right * scale)

    left, right = lax.fori_loop(0, size, eliminate, (block, eye))
    pivots = jnp.sum(jnp.where(row_ids == lane_ids, left, 0.0), axis=1, keepdims=True)
    scale = 1.0 / jnp.sqrt(pivots)
    upper = jnp.where(lane_ids >= row_ids, left * scale, 0.0)
    return upper.T, jnp.where(lane_ids <= row_ids, right * scale, 0.0)


def factor_tile(work, factor, inverse):
    size = work.shape[0]
    factor[...] = jnp.zeros_like(factor)
    inverse[...] = jnp.zeros_like(inverse)
    for start in range(0, size, BLOCK):
        end = start + BLOCK
        here = slice(start, end)
        lower, back = factor_block(work[here, here])
        factor[here, here] = lower
        inverse[here, here] = back
        if start:
            so_far = exact(factor[here, :start], inverse[:start, :start], NN)
            inverse[here, :start] = -exact(back, so_far, NN)
        if end < size:
            panel = exact(work[end:, here], back, NT)
            factor[end:, here] = panel
            work[end:, end:] = work[end:, end:] - exact(panel, panel, NT)


def factor_kernel(seeds, factors, inverses, link, work):
    work[...] = seeds[0]
    factor_tile(work, factors.at[0], inverses.at[0])
    link[...] = exact(seeds[1], inverses[0], NT)
    work[...] = seeds[2] - exact(link[...], link[...], NT)
    factor_tile(work, factors.at[1], inverses.at[1])


def panel_kernel(table, raw0, raw1, inverses, link, high, low, parts_high, parts_low):
    e = pl.program_id(0)
    tile = link.shape[0]

    @pl.when(e == 0)
    def _():
        for at, value in ((0, inverses[0]), (1, inverses[1]), (2, link[...])):
            hi, lo = split(value)
            parts_high[at] = hi
            parts_low[at] = lo

    first = three(*split(raw0[...]), parts_high[0], parts_low[0])
    first = jnp.where(table[1, e] > 0, first, 0.0)
    hi, lo = split(first)
    high[:, :tile] = hi
    low[:, :tile] = lo
    second = raw1[...] - three(hi, lo, parts_high[2], parts_low[2])
    hi, lo = split(three(*split(second), parts_high[1], parts_low[1]))
    high[:, tile:] = hi
    low[:, tile:] = lo


def update_kernel(table, local, high, low, factors, out):
    e = pl.program_id(0)
    mode = table[0, e]
    mine = table[1, e]
    across = table[2, e]
    step = table[3, e]
    tile = local.shape[0]

    @pl.when(mode == 0)
    def _():
        out[...] = local[...]

    @pl.when(mode == 1)
    def _():
        out[...] = local[...] - three(high[mine], low[mine], high[across], low[across])

    for k in range(STEPS):
        @pl.when(jnp.logical_and(mode == 2, step == k))
        def _():
            cut = slice(k * tile, (k + 1) * tile)
            out[...] = high[mine, :, cut].astype(jnp.float32) + low[mine, :, cut].astype(jnp.float32)

    @pl.when(mode == 3)
    def _():
        out[...] = factors[step]


def shards(band):
    slots, _, groups, _, tile, _ = band.shape
    n = lax.axis_size("row")
    grid_cols = lax.axis_size("col")
    bandt = slots * n
    r = lax.axis_index("row")
    c = lax.axis_index("col")
    f32 = jnp.float32
    local = band.reshape(slots, groups, tile, tile)
    dma = pltpu.SemaphoreType.DMA
    anywhere = pl.BlockSpec(memory_space=pl.ANY)
    in_vmem = pl.BlockSpec(memory_space=pltpu.VMEM)
    entries = slots + groups
    limit = 56 * 1024 * 1024

    rows, seeds = pl.pallas_call(
        spread_kernel,
        out_shape=(jax.ShapeDtypeStruct((STEPS, entries, tile, tile), f32), jax.ShapeDtypeStruct((3, tile, tile), f32)),
        in_specs=[anywhere],
        out_specs=(anywhere, anywhere),
        scratch_shapes=[dma((slots,)), dma((slots,)), dma((slots,)), dma((slots,)), dma((STEPS, groups)),
                        dma((STEPS, groups)), dma((STEPS, groups)), dma((3, n)), dma((3,))],
        compiler_params=pltpu.CompilerParams(collective_id=0, has_side_effects=True),
        name="spread_columns",
    )(local)

    square = jax.ShapeDtypeStruct((STEPS, tile, tile), f32)
    factors, inverses, link = pl.pallas_call(
        factor_kernel,
        out_shape=(square, square, jax.ShapeDtypeStruct((tile, tile), f32)),
        in_specs=[in_vmem],
        out_specs=(in_vmem, in_vmem, in_vmem),
        scratch_shapes=[pltpu.VMEM((tile, tile), f32)],
        compiler_params=pltpu.CompilerParams(vmem_limit_bytes=limit),
        name="factor_diagonals",
    )(seeds)

    entry = jnp.arange(entries, dtype=jnp.int32)
    group_of = jnp.maximum(entry - slots, 0)
    row_of = jnp.where(entry < slots, 1 + entry * n + (r - 1) % n, group_of * grid_cols + c)
    source = jnp.where(entry < slots, jnp.minimum(row_of // n, slots - 1), entry)
    table = jnp.stack([source, (row_of < bandt).astype(jnp.int32)])
    half = jax.ShapeDtypeStruct((entries, tile, STEPS * tile), jnp.bfloat16)
    once = pl.Buffered(1)
    high, low = pl.pallas_call(
        panel_kernel,
        out_shape=(half, half),
        grid_spec=pltpu.PrefetchScalarGridSpec(
            num_scalar_prefetch=1,
            grid=(entries,),
            in_specs=[
                pl.BlockSpec((None, None, tile, tile), lambda e, t: (0, t[0, e], 0, 0)),
                pl.BlockSpec((None, None, tile, tile), lambda e, t: (1, e, 0, 0)),
                pl.BlockSpec((STEPS, tile, tile), lambda e, t: (0, 0, 0), pipeline_mode=once),
                pl.BlockSpec((tile, tile), lambda e, t: (0, 0), pipeline_mode=once),
            ],
            out_specs=[pl.BlockSpec((None, tile, STEPS * tile), lambda e, t: (e, 0, 0))] * 2,
            scratch_shapes=[pltpu.VMEM((3, tile, tile), jnp.bfloat16)] * 2,
        ),
        compiler_params=pltpu.CompilerParams(vmem_limit_bytes=limit),
        name="panels",
    )(table, rows, rows, inverses, link)

    count = slots * groups
    at = jnp.arange(count, dtype=jnp.int32)
    slot = at // groups
    group = at % groups
    column = group * grid_cols + c
    row = column + slot * n + (r - column) % n
    mode = jnp.where(column < STEPS, jnp.where(row == column, 3, 2), jnp.where(row <= bandt, 1, 0))
    step = jnp.minimum(column, STEPS - 1)
    mine = jnp.clip((row + n - 1) // n - 1, 0, slots - 1)
    table = jnp.stack([mode, mine, slots + group, step]).astype(jnp.int32)
    whole = pl.BlockSpec((entries, tile, STEPS * tile), lambda e, t: (0, 0, 0), pipeline_mode=once)
    block = pl.BlockSpec((None, None, tile, tile), lambda e, t: (e // groups, e % groups, 0, 0))
    out = pl.pallas_call(
        update_kernel,
        out_shape=jax.ShapeDtypeStruct(local.shape, f32),
        grid_spec=pltpu.PrefetchScalarGridSpec(
            num_scalar_prefetch=1,
            grid=(count,),
            in_specs=[block, whole, whole,
                      pl.BlockSpec((STEPS, tile, tile), lambda e, t: (0, 0, 0), pipeline_mode=once)],
            out_specs=block,
        ),
        compiler_params=pltpu.CompilerParams(vmem_limit_bytes=limit),
        name="updates",
    )(table, local, high, low, factors)
    return out.reshape(slots, 1, groups, 1, tile, tile)


def solution(mesh):
    return jax.shard_map(
        shards,
        mesh=mesh,
        in_specs=(P(None, "row", None, "col", None, None),),
        out_specs=P(None, "row", None, "col", None, None),
        check_vma=False,
    )
```

time: 1360 us -> 816 us (0.60); the launches traced: 1340 us -> 815 us
  Pallas kernels: 0 us -> 814 us
  waiting for transfers between devices: 666 us -> 0 us
  other arithmetic: 328 us -> 1.25 us
  matrix products: 183 us -> 0 us
  local copies, waits for them, and re-layouts: 145 us -> 0 us
  between operations: 19.6 us -> 0.02 us
    pallas_call x0 -> x4, Pallas kernels: none -> 814 us  [the longest x1 575 us: shards(): pl.pallas_call(spread_kernel, out_shape=(jax.ShapeDtypeStruct((STEPS, ent...]
    psum x6 -> x0, waiting for transfers between devices: 666 us -> none  [spread(): return lax.psum(jnp.where(mine, x, jnp.zeros_like(x)), axis)]
    another operation x34 -> x2, other arithmetic: 240 us -> 1.19 us  [the longest x1 0.6 us: shards(): table = jnp.stack([source, (row_of < bandt).astype(jnp.int32)])]
    dot_general x4 -> x0, matrix products: 168 us -> none  [the longest x2 128 us: shards(): update = jnp.einsum('sqab,qcb->sqac', gathered, across, precision=highest)]
    select_n x7 -> x2, other arithmetic: 58.3 us -> 0.04 us  [the longest x1 0.03 us: shards(): jnp.where(column < STEPS, jnp.where(row == column, 3, 2), jnp.where(row <...]
    unnamed x3 -> x0, local copies, waits for them, and re-layouts: 34.3 us -> none
    reshape x1 -> x0, local copies, waits for them, and re-layouts: 34.1 us -> none  [shards(): return local.reshape(slots, 1, colgroups, 1, tile, tile)]
    gather x2 -> x0, local copies, waits for them, and re-layouts: 33.6 us -> none  [shards(): jnp.take(slab, wanted.reshape(-1), axis=0)]
  transfers between devices with their start and end apart: 6 -> 0, of which waited for: 6 -> 0; matrix products, arithmetic and copies ran while one was open for 9% -> 0% of each run, Pallas kernels for 0% -> 0%
where the time goes in v1:
time: 816 us; the launch traced here: 815 us
  Pallas kernels  814 us (100%)
    pallas_call x1, Pallas kernels, shards(): pl.pallas_call(spread_kernel, out_shape=(jax.ShapeDtypeStruct((STEPS, ent...  575 us
    pallas_call x1, Pallas kernels, shards(): pl.pallas_call(factor_kernel, out_shape=(square, square, jax.ShapeDtypeSt...  144 us
    pallas_call x1, Pallas kernels, shards(): pl.pallas_call(update_kernel, out_shape=jax.ShapeDtypeStruct(local.shape,...  57 us
    pallas_call x1, Pallas kernels, shards(): pl.pallas_call(panel_kernel, out_shape=(half, half), grid_spec=pltpu.Pref...  37.9 us

profile of v1, /device:TPU:3, one launch (start us, length us, event | category | flops | bytes accessed | tf_op | source)
XLA Modules:
  0.0 815.5 jit_solution(8426426078473945292)
XLA Ops:
  0.0 0.6 pad_add_fusion.1.table
  0.7 0.6 pad_add_fusion.table
  1.3 575.4 %spread_columns.1 = (f32[2,12,512,512]{3,2,1,0:T(8,128)}, f32[3,512,512]{2,1,0:T(8,128)}) custom-call(f32[8,4,512,512]{3,2,1,0:T(8,128)} %bitcast.4), custom_call_target="tpu_custom_call" | custom-call | tf_op jit(solution)/shard_map/spread_columns/pallas_call | solution.py:287
  576.6 143.9 %factor_diagonals.1 = (f32[2,512,512]{2,1,0:T(8,128)}, f32[2,512,512]{2,1,0:T(8,128)}, f32[512,512]{1,0:T(8,128)}) custom-call(f32[3,512,512]{2,1,0:T(8,128)} %get-tuple-element.13.seeds), custom_call_target="tpu_custom_call" | custom-call | tf_op jit(solution)/shard_map/factor_diagonals/pallas_call | solution.py:299
  720.6 37.9 %panels.1 = (bf16[12,512,1024]{2,1,0:T(8,128)(2,1)}, bf16[12,512,1024]{2,1,0:T(8,128)(2,1)}) custom-call(s32[2,12]{1,0:T(2,128)} %pad_add_fusion.1.table, f32[2,12,512,512]{3,2,1,0:T(8,128)} %get-tuple-element.12.raw0.raw1, f32[2,12,512,512]{3,2,1,0:T(8,128)} %get-tuple-element.12.raw0.raw1, f32[2,512,512]{2,1,0:T(8,128)} %get-tuple-element.14.inverses, ...), custom_call_target="tpu_custom_call" | custom-call | tf_op jit(solution)/shard_map/panels/pallas_call | solution.py:316
  758.5 57.0 %updates.1 = f32[8,4,512,512]{3,2,1,0:T(8,128)} custom-call(s32[4,32]{1,0:T(4,128)} %pad_add_fusion.table, f32[8,4,512,512]{3,2,1,0:T(8,128)} %bitcast.5, bf16[12,512,1024]{2,1,0:T(8,128)(2,1)} %get-tuple-element.16.high, bf16[12,512,1024]{2,1,0:T(8,128)(2,1)} %get-tuple-element.17.low, f32[2,512,512]{2,1,0:T(8,128)} %get-tuple-element.18.factors), custom_call_target="tpu_custom_call" | custom-call | tf_op jit(solution)/shard_map/updates/pallas_call | solution.py:347
  (4 shorter events, 0.1 us)
